TPU v7x, 32 devices: a whole 2x2x4 slice. The times are simulated.
32 devices in a mesh: parts: 2 (over x), blk: 8 (over z, y), kvh: 2 (over core).
Axes of the slice: x: 2, y: 2, z: 4, core: 2. Of those that a mesh axis runs over, the one named last changes fastest.
Arguments:
- queries: bfloat16 [512, 5120], P(('parts', 'blk'), 'kvh'), parts along dimension 0, may hold values from -20 to 20
- block_key_cache: bfloat16 [128, 512, 1024], P(('parts', 'blk'), None, 'kvh'), parts along dimension 0, may hold values from -5 to 5
- block_value_cache: bfloat16 [128, 512, 1024], P(('parts', 'blk'), None, 'kvh'), parts along dimension 0, may hold values from -12 to 12
- new_keys: bfloat16 [512, 1024], P(('parts', 'blk'), 'kvh'), parts along dimension 0, may hold values from -9 to 9
- leaf_value_rows: bfloat16 [512, 1024], P(('parts', 'blk'), 'kvh'), parts along dimension 0, may hold values from -12 to 12
- ancestors: int32 [512, 8], P(('parts', 'blk')), parts along dimension 0, may hold values from 0 to 63, as said below
- block_slot: int32 [128], P('parts'), parts along dimension 0, may hold values from 0 to 63, as said below
- last_len: int32 [512], P(('parts', 'blk')), parts along dimension 0, may hold values from 1 to 512
- o_weight: bfloat16 [5120, 5120], P('kvh', 'blk'), may hold values from -0.078125 to 0.078125
Outputs:
- mixed: bfloat16 [512, 5120], P(('parts', 'kvh'), 'blk'), parts along dimension 0
There are 2 independent parts, one for each index of `parts`. A program takes and returns all parts, laid end to end along the dimension named above; an argument that names none is the same for every part. Nothing has to cross between parts.
Inputs may be any that keep to these rules, and one draw needn't show every extreme that they name: `ancestors`: each row names 8 different blocks; the 32 rows of one device name no block more than 8 times. `block_slot`: A permutation: each block has its own row of the caches.
All inputs are finite; a program needn't handle non-finite values.
Results may differ from a plain program's by a relative error of at most 0.0051.
Values may be sent and summed in bfloat16 or wider, within the bound.
A program may use at most 128 MiB of HBM per device.

v0:
```python
import math

import jax
import jax.numpy as jnp
from jax import lax
from jax.sharding import PartitionSpec as P

QUERY_HEADS = 40
KEY_VALUE_HEADS = 8
HEAD_SIZE = 128


def slot_lookup(ancestors, block_slot):
    block_count = block_slot.shape[0]
    catalog = jnp.arange(block_count, dtype=jnp.int32)
    flat_ids = ancestors.reshape(-1)
    matches = flat_ids[:, None] == catalog[None, :]
    return jnp.sum(jnp.where(matches, block_slot[None, :], 0), axis=1)


def slot_ranks(slot_row_list):
    pair_count = slot_row_list.shape[-1]
    ordinal = jnp.arange(pair_count, dtype=jnp.int32)
    earlier = ordinal[None, :] < ordinal[:, None]
    same_slot = slot_row_list[..., :, None] == slot_row_list[..., None, :]
    return jnp.sum(same_slot & earlier, axis=-1)


def pair_lengths(last_len, ancestry, block_len):
    levels = jnp.arange(ancestry, dtype=jnp.int32)
    return jnp.where(levels[None, :] == ancestry - 1, last_len[:, None], block_len).reshape(-1)


def owner_attention(query_buffer, length_buffer, block_key_cache, block_value_cache, score_scale):
    sources, width_rows, features = query_buffer.shape
    local_blocks, block_len, kv_features = block_key_cache.shape
    capacity = width_rows // local_blocks
    kv_local = kv_features // HEAD_SIZE
    queries_per_group = QUERY_HEADS // KEY_VALUE_HEADS
    arranged = jnp.moveaxis(
        query_buffer.reshape(
            sources, local_blocks, capacity, kv_local, queries_per_group, HEAD_SIZE
        ),
        1,
        0,
    )
    counted = jnp.moveaxis(length_buffer.reshape(sources, local_blocks, capacity), 1, 0)
    gathered_keys = block_key_cache.reshape(local_blocks, block_len, kv_local, HEAD_SIZE)
    gathered_values = block_value_cache.reshape(local_blocks, block_len, kv_local, HEAD_SIZE)
    positions = jnp.arange(block_len, dtype=jnp.int32)

    def one_block(block_items):
        query_part, count_part, key_part, value_part = block_items
        scores = (
            jnp.einsum("scgeh,kgh->gscek", query_part, key_part, preferred_element_type=jnp.float32)
            * score_scale
        )
        in_block = positions[None, None, :] < count_part[:, :, None]
        scores = jnp.where(in_block[None, :, :, None, :], scores, -1e30)
        block_max = jnp.max(scores, axis=-1)
        shares = jnp.exp(scores - block_max[..., None]).astype(jnp.bfloat16)
        row_total = jnp.sum(shares, axis=-1, dtype=jnp.float32)
        partial_value = jnp.einsum(
            "gscek,kgh->scgeh", shares, value_part, preferred_element_type=jnp.float32
        )
        totals_here = jnp.transpose(row_total, (1, 2, 0, 3))
        unit = (partial_value / totals_here[..., None]).astype(jnp.bfloat16)
        return (unit, jnp.transpose(block_max, (1, 2, 0, 3)), totals_here)

    unit, block_max, row_total = lax.map(
        one_block, (arranged, counted, gathered_keys, gathered_values)
    )
    unit = jnp.moveaxis(unit, 0, 1).reshape(sources, width_rows, features)
    block_max = jnp.moveaxis(block_max, 0, 1).reshape(
        sources, width_rows, kv_local * queries_per_group
    )
    row_total = jnp.moveaxis(row_total, 0, 1).reshape(
        sources, width_rows, kv_local * queries_per_group
    )
    return (unit, block_max, row_total)


def local(
    queries,
    block_key_cache,
    block_value_cache,
    new_keys,
    leaf_value_rows,
    ancestors,
    block_slot,
    last_len,
    o_weight,
):
    leaf_count, features = queries.shape
    ancestry = ancestors.shape[1]
    local_blocks, block_len, kv_features = block_key_cache.shape
    devices_blk = lax.axis_size("blk")
    block_count = local_blocks * devices_blk
    capacity = 2 * leaf_count * ancestry // block_count
    kv_local = kv_features // HEAD_SIZE
    queries_per_group = QUERY_HEADS // KEY_VALUE_HEADS
    heads_local = kv_local * queries_per_group
    score_scale = 1.0 / math.sqrt(HEAD_SIZE)
    buffer_rows = block_count * capacity
    slot_row_list = slot_lookup(ancestors, block_slot)
    destination = slot_row_list * capacity + slot_ranks(slot_row_list)
    pair_leaf = jnp.arange(leaf_count * ancestry, dtype=jnp.int32) // ancestry
    leaf_index = jnp.zeros((buffer_rows,), jnp.int32).at[destination].set(pair_leaf)
    length_flat = (
        jnp.zeros((buffer_rows,), jnp.int32)
        .at[destination]
        .set(pair_lengths(last_len, ancestry, block_len))
    )
    outgoing = queries[leaf_index].reshape(devices_blk, local_blocks * capacity, features)
    query_buffer, length_buffer = (
        lax.all_to_all(outgoing, "blk", split_axis=0, concat_axis=0, tiled=True),
        lax.all_to_all(
            length_flat.reshape(devices_blk, local_blocks * capacity),
            "blk",
            split_axis=0,
            concat_axis=0,
            tiled=True,
        ),
    )
    unit, block_max, row_total = owner_attention(
        query_buffer, length_buffer, block_key_cache, block_value_cache, score_scale
    )
    unit = lax.all_to_all(unit, "blk", split_axis=0, concat_axis=0, tiled=True)
    block_max, row_total = (
        lax.all_to_all(block_max, "blk", split_axis=0, concat_axis=0, tiled=True),
        lax.all_to_all(row_total, "blk", split_axis=0, concat_axis=0, tiled=True),
    )
    unit = unit.reshape(buffer_rows, features)[destination].reshape(
        leaf_count, ancestry, kv_local, queries_per_group, HEAD_SIZE
    )
    block_max = block_max.reshape(buffer_rows, heads_local)[destination].reshape(
        leaf_count, ancestry, kv_local, queries_per_group
    )
    row_total = row_total.reshape(buffer_rows, heads_local)[destination].reshape(
        leaf_count, ancestry, kv_local, queries_per_group
    )
    head_row_block = queries.reshape(leaf_count, kv_local, queries_per_group, HEAD_SIZE)
    own_token_score = (
        jnp.einsum(
            "lgeh,lgh->lge",
            head_row_block,
            new_keys.reshape(leaf_count, kv_local, HEAD_SIZE),
            preferred_element_type=jnp.float32,
        )
        * score_scale
    )
    overall = jnp.maximum(jnp.max(block_max, axis=1), own_token_score)
    weights = jnp.exp(block_max - overall[:, None]) * row_total
    own_token_weight = jnp.exp(own_token_score - overall)
    weighted_numerator = jnp.sum(weights[..., None] * unit.astype(jnp.float32), axis=1)
    weighted_numerator = weighted_numerator + own_token_weight[..., None] * leaf_value_rows.reshape(
        leaf_count, kv_local, 1, HEAD_SIZE
    ).astype(jnp.float32)
    denominator = jnp.sum(weights, axis=1) + own_token_weight
    attention = (
        (weighted_numerator / denominator[..., None])
        .reshape(leaf_count, features)
        .astype(jnp.bfloat16)
    )
    columns = jnp.dot(
        lax.all_gather(attention, "blk", axis=0, tiled=True),
        o_weight,
        preferred_element_type=jnp.float32,
    )
    return lax.psum_scatter(columns, "kvh", scatter_dimension=0, tiled=True).astype(jnp.bfloat16)


def solution(mesh):
    return jax.shard_map(
        local,
        mesh=mesh,
        in_specs=(
            P(("parts", "blk"), "kvh"),
            P(("parts", "blk"), None, "kvh"),
            P(("parts", "blk"), None, "kvh"),
            P(("parts", "blk"), "kvh"),
            P(("parts", "blk"), "kvh"),
            P(("parts", "blk"), None),
            P("parts"),
            P(("parts", "blk")),
            P("kvh", "blk"),
        ),
        out_specs=P(("parts", "kvh"), "blk"),
        check_vma=False,
    )
```

profile of v0, /device:TPU:0, one launch (start us, length us, event | category | flops | bytes accessed | tf_op | source)
XLA Modules:
  0.0 298.2 jit_solution(15268052671273725230)
XLA Ops:
  11.4 7.3 %all-to-all-start = ((s32[8,1,64]{2,1,0:T(1,128)}), s32[8,1,64]{2,1,0:T(1,128)S(1)}, u32[]{:S(2)}, u32[]{:S(2)}) async-start(s32[8,1,64]{2,1,0:T(1,128)} %all_to_all.18), calls=%async_computation | async-start | bytes 8192 | tf_op jit(solution)/shard_map/all_to_all | solution.py:117
  20.1 7.1 %gather_fusion = bf16[512,2560]{1,0:T(8,128)(2,1)} fusion(bf16[32,2560]{1,0:T(8,128)(2,1)} %param.11, s32[1024]{0:T(1024)S(1)} %pad_clamp_fusion.1), kind=kCustom, calls=%fused_computation | custom fusion | bytes 5244928 | tf_op jit(solution)/shard_map/gather | solution.py:114
  27.2 6.0 %all-to-all-start.1 = ((bf16[8,64,2560]{2,1,0:T(8,128)(2,1)}), bf16[8,64,2560]{2,1,0:T(8,128)(2,1)}, u32[]{:S(2)}, u32[]{:S(2)}) async-start(bf16[8,64,2560]{2,1,0:T(8,128)(2,1)} %bitcast.110), calls=%async_computation.1 | async-start | bytes 5242880 | tf_op jit(solution)/shard_map/all_to_all | solution.py:116
  33.2 6.5 %copy.47 = bf16[8,512,512]{1,2,0:T(8,128)(2,1)} copy(bf16[8,512,512]{2,1,0:T(8,128)(2,1)} %param.13) | data formatting | bytes 8388608 | tf_op args[2]
  39.7 6.5 %copy.49 = bf16[8,512,512]{1,2,0:T(8,128)(2,1)} copy(bf16[8,512,512]{2,1,0:T(8,128)(2,1)} %param.12) | data formatting | bytes 8388608 | tf_op args[1]
  47.4 44.8 %all-to-all-done.1 = bf16[8,64,2560]{2,1,0:T(8,128)(2,1)} async-done(((bf16[8,64,2560]{2,1,0:T(8,128)(2,1)}), bf16[8,64,2560]{2,1,0:T(8,128)(2,1)}, u32[]{:S(2)}, u32[]{:S(2)}) %all-to-all-start.1) | async-done | bytes 2621472 | tf_op jit(solution)/shard_map/all_to_all | solution.py:116
  92.2 48.9 %while.15 = (s32[]{:T(128)}, bf16[8,8,8,4,5,128]{5,2,4,3,0,1:T(8,128)(2,1)}, f32[8,8,8,4,5]{2,4,1,3,0:T(8,128)}, f32[8,8,8,4,5]{2,4,1,3,0:T(8,128)}, bf16[8,512,...) while((s32[]{:T(128)}, ...), condition=%wide.region_7.8_spmd.clone, body=%wide.region_4.7_spmd.clone.sunk | while | flops 344421888 | bytes 10654581 | solution.py:70
  94.9 1.9 fusion.33
  101.0 1.9 fusion.33
  113.2 1.9 fusion.33
  119.3 1.9 fusion.33
  137.7 1.9 fusion.33
  141.1 2.4 copy.71
  145.6 3.6 %all-to-all-start.3 = ((f32[8,1,1280]{2,1,0:T(1,128)}), f32[8,1,1280]{2,1,0:T(1,128)S(1)}, u32[]{:S(2)}, u32[]{:S(2)}) async-start(f32[8,1,1280]{2,1,0:T(1,128)} %reshape.220), calls=%async_computation.3 | async-start | bytes 81920 | tf_op jit(solution)/shard_map/all_to_all | solution.py:131
  149.2 2.4 copy.70
  153.1 2.9 all-to-all-done.3
  156.0 9.8 %all_to_all.29 = f32[8,1,1280]{2,1,0:T(1,128)} all-to-all(f32[8,1,1280]{2,1,0:T(1,128)S(1)} %reshape.222), channel_id=1, replica_groups=mesh['parts'=2,'blk'=8,'kvh'=2] {'blk'}, dimensions={0} | all-to-all | bytes 81920 | tf_op jit(solution)/shard_map/all_to_all | solution.py:130
  165.7 4.5 %all-to-all-start.4 = ((bf16[8,64,2560]{2,1,0:T(8,128)(2,1)}), bf16[8,64,2560]{2,1,0:T(8,128)(2,1)}, u32[]{:S(2)}, u32[]{:S(2)}) async-start(bf16[8,64,2560]{2,1,0:T(8,128)(2,1)} %bitcast.115), calls=%async_computation.4 | async-start | bytes 5242880 | tf_op jit(solution)/shard_map/all_to_all | solution.py:128
  192.9 35.3 %all-to-all-done.4 = bf16[8,64,2560]{2,1,0:T(8,128)(2,1)} async-done(((bf16[8,64,2560]{2,1,0:T(8,128)(2,1)}), bf16[8,64,2560]{2,1,0:T(8,128)(2,1)}, u32[]{:S(2)}, u32[]{:S(2)}) %all-to-all-start.4) | async-done | bytes 2621472 | tf_op jit(solution)/shard_map/all_to_all | solution.py:128
  228.2 6.0 %gather_fusion.3 = bf16[256,2560]{1,0:T(8,128)(2,1)} fusion(bf16[512,2560]{1,0:T(8,128)(2,1)} %bitcast.15, s32[1024]{0:T(1024)} %pad_clamp_fusion), kind=kCustom, calls=%fused_computation.3 | custom fusion | bytes 2622464 | tf_op jit(solution)/shard_map/gather | solution.py:133
  234.2 2.1 fusion.13
  238.5 40.9 %all-gather.2.cloned.1.call-done = bf16[256,2560]{1,0:T(8,128)(2,1)} async-done(((bf16[32,2560]{1,0:T(8,128)(2,1)}), bf16[256,2560]{1,0:T(8,128)(2,1)}) %all-gather.2.cloned.1.call-update) | async-done | bytes 1310736 | tf_op jit(solution)/shard_map/all_gather | solution.py:166
  279.4 3.4 %fusion.23 = f32[256,640]{1,0:T(8,128)} fusion(bf16[256,2560]{1,0:T(8,128)(2,1)} %all-gather.2.cloned.1.call-done, bf16[2560,640]{1,0:T(8,128)(2,1)S(1)} %copy-done), kind=kOutput, calls=%fused_computation.59 | convolution fusion | flops 838860800 | bytes 5242880 | tf_op jit(solution)/shard_map/dot_general | solution.py:165
  282.8 6.9 %reduce-scatter.2.cloned.1.call-done = f32[128,640]{1,0:T(8,128)} async-done(((f32[256,640]{1,0:T(8,128)}), f32[128,640]{1,0:T(8,128)}) %reduce-scatter.2.cloned.1.call-update) | async-done | bytes 327696 | tf_op jit(solution)/shard_map/reduce_scatter | solution.py:170
  (116 shorter events, 76.5 us)
Async XLA Ops:
  6.5 272.9 %copy-start = (bf16[2560,640]{1,0:T(8,128)(2,1)S(1)}, bf16[2560,640]{1,0:T(8,128)(2,1)}, u32[]{:S(2)}) copy-start(bf16[2560,640]{1,0:T(8,128)(2,1)} %param.19) | copy-start | bytes 9830404
  11.4 15.8 %all-to-all-start = ((s32[8,1,64]{2,1,0:T(1,128)}), s32[8,1,64]{2,1,0:T(1,128)S(1)}, u32[]{:S(2)}, u32[]{:S(2)}) async-start(s32[8,1,64]{2,1,0:T(1,128)} %all_to_all.18), calls=%async_computation | async-start | bytes 8192 | tf_op jit(solution)/shard_map/all_to_all | solution.py:117
  27.2 65.0 %all-to-all-start.1 = ((bf16[8,64,2560]{2,1,0:T(8,128)(2,1)}), bf16[8,64,2560]{2,1,0:T(8,128)(2,1)}, u32[]{:S(2)}, u32[]{:S(2)}) async-start(bf16[8,64,2560]{2,1,0:T(8,128)(2,1)} %bitcast.110), calls=%async_computation.1 | async-start | bytes 5242880 | tf_op jit(solution)/shard_map/all_to_all | solution.py:116
  145.6 10.4 %all-to-all-start.3 = ((f32[8,1,1280]{2,1,0:T(1,128)}), f32[8,1,1280]{2,1,0:T(1,128)S(1)}, u32[]{:S(2)}, u32[]{:S(2)}) async-start(f32[8,1,1280]{2,1,0:T(1,128)} %reshape.220), calls=%async_computation.3 | async-start | bytes 81920 | tf_op jit(solution)/shard_map/all_to_all | solution.py:131
  165.7 4.8 %copy-start.1 = (bf16[32,2560]{1,0:T(8,128)(2,1)S(1)}, bf16[32,2560]{1,0:T(8,128)(2,1)}, u32[]{:S(2)}) copy-start(bf16[32,2560]{1,0:T(8,128)(2,1)} %param.11) | copy-start | bytes 491524
  165.7 5.7 %copy-start.2 = (bf16[32,512]{1,0:T(8,128)(2,1)S(1)}, bf16[32,512]{1,0:T(8,128)(2,1)}, u32[]{:S(2)}) copy-start(bf16[32,512]{1,0:T(8,128)(2,1)} %param.14) | copy-start | bytes 98308
  165.7 62.4 %all-to-all-start.4 = ((bf16[8,64,2560]{2,1,0:T(8,128)(2,1)}), bf16[8,64,2560]{2,1,0:T(8,128)(2,1)}, u32[]{:S(2)}, u32[]{:S(2)}) async-start(bf16[8,64,2560]{2,1,0:T(8,128)(2,1)} %bitcast.115), calls=%async_computation.4 | async-start | bytes 5242880 | tf_op jit(solution)/shard_map/all_to_all | solution.py:128
  170.3 109.2 %all-gather.2.cloned.1.call-start = ((), (), s32[]{:S(2)}) async-start(), calls=%async_computation.6 | async-start | bytes 1474560 | tf_op jit(solution)/shard_map/all_gather | solution.py:166
  238.5 51.3 %reduce-scatter.2.cloned.1.call-start = ((), (), s32[]{:S(2)}) async-start(), calls=%async_computation.7 | async-start | bytes 983040 | tf_op jit(solution)/shard_map/reduce_scatter | solution.py:170
Sparse Core Ops, SparseCore 0:
  238.6 40.7 all-gather.1
  282.9 6.7 reduce-scatter.1
where the time goes:
time: 300 us; the launch traced here: 298 us
  waiting for transfers between devices  131 us (44%)
  local copies, waits for them, and re-layouts  68.5 us (23%)
  matrix products  33.8 us (11%)
  starting transfers between devices  21.7 us (7%)
  other arithmetic  19.8 us (7%)
  between operations  13.6 us (5%)
  blocking collectives  9.79 us (3%)
    all_to_all x1, waiting for transfers between devices, local(): lax.all_to_all(outgoing, 'blk', split_axis=0, concat_axis=0, tiled=True)  44.8 us
    all_gather x1, waiting for transfers between devices, local(): lax.all_gather(attention, 'blk', axis=0, tiled=True)  40.9 us
    all_to_all x1, waiting for transfers between devices, local(): unit = lax.all_to_all(unit, 'blk', split_axis=0, concat_axis=0, tiled=True)  35.3 us
    unnamed x13, local copies, waits for them, and re-layouts  16.1 us
    dot_general x8, matrix products, one_block(): jnp.einsum('gscek,kgh->scgeh', shares, value_part, preferred_element_type...  15.2 us
    dot_general x8, matrix products, one_block(): jnp.einsum('scgeh,kgh->gscek', query_part, key_part, preferred_element_ty...  14 us
    dynamic_update_slice x16, local copies, waits for them, and re-layouts, owner_attention(): lax.map(one_block, (arranged, counted, gathered_keys, gathered_values))  12.3 us
    all_to_all x1, blocking collectives, local(): lax.all_to_all(block_max, 'blk', split_axis=0, concat_axis=0, tiled=True)  9.79 us
  transfers between devices with their start and end apart: 6, of which 5 were waited for; matrix products, arithmetic and copies ran while one was open for 16% of the time, Pallas kernels for 0%

commit v1 on v0

v1 whole, which is shorter than its diff:
```python
import functools
import math

import jax
import jax.numpy as jnp
from jax import lax
from jax.experimental import pallas as pl
from jax.experimental.pallas import tpu as pltpu
from jax.sharding import PartitionSpec as P

QUERY_HEADS = 40
KEY_VALUE_HEADS = 8
HEAD_SIZE = 128
PER_GROUP = QUERY_HEADS // KEY_VALUE_HEADS
ROW_PAIR = 2
SLICES = 1
NEG = -1e30
MESH = pl.DeviceIdType.MESH
F32 = jnp.float32
BF16 = jnp.bfloat16


def dot(a, b):
    return jnp.dot(a, b, preferred_element_type=F32)


def kernel(
    n,
    slices,
    cap,
    q_ref,
    info_ref,
    nk_ref,
    nv_ref,
    key_hbm,
    value_hbm,
    weight_hbm,
    out_ref,
    info_buf,
    q_buf,
    key_buf,
    value_buf,
    weight_buf,
    pick,
    pick_t,
    count,
    unit_buf,
    max_buf,
    total_buf,
    part,
    y_recv,
    merged,
    z_recv,
    att_buf,
    half_send,
    half_recv,
    kv_sem,
    w_sem,
    g_recv,
    g_up,
    g_down,
    g_side,
    y_send_sem,
    y_recv_sem,
    z_send_sem,
    z_recv_sem,
    h_send_sem,
    h_recv_sem,
):
    parts_at = lax.axis_index("parts")
    me = lax.axis_index("blk")
    core = lax.axis_index("kvh")
    nz = n // ROW_PAIR
    z = me // ROW_PAIR
    y = me % ROW_PAIR
    other_y = 1 - y
    leaves = q_ref.shape[0]
    all_leaves = n * leaves
    blocks, block_len, kv_width = key_hbm.shape
    groups = kv_width // HEAD_SIZE
    sg = groups // slices
    heads = sg * PER_GROUP
    width = heads * HEAD_SIZE
    scale = 1.0 / math.sqrt(HEAD_SIZE)
    scale2 = scale * math.log2(math.e)

    def where_is(zz, yy):
        return (parts_at, zz * ROW_PAIR + yy, core)

    kv_copies = []
    for b in range(blocks):
        kv_copies.append(
            (
                pltpu.make_async_copy(key_hbm.at[b], key_buf.at[b], kv_sem.at[0, b]),
                pltpu.make_async_copy(value_hbm.at[b], value_buf.at[b], kv_sem.at[1, b]),
            )
        )

    info_buf[0, me] = info_ref[...]
    for s in range(slices):
        q_buf[s, me] = q_ref[:, s * width : (s + 1) * width]

    barrier = pltpu.get_barrier_semaphore()
    for d in range(1, nz):
        pl.semaphore_signal(
            barrier, inc=1, device_id=where_is((z + d) % nz, y), device_id_type=MESH
        )
    pl.semaphore_signal(barrier, inc=1, device_id=where_is(z, other_y), device_id_type=MESH)
    pl.semaphore_signal(barrier, inc=1, device_id=(parts_at, me, 1 - core), device_id_type=MESH)
    pl.semaphore_wait(barrier, nz + 1)

    def gather_copy(buf, s, row, zz, yy, target, send_sem):
        idx = zz * ROW_PAIR + yy
        return pltpu.make_async_remote_copy(
            src_ref=buf.at[s, idx],
            dst_ref=buf.at[s, idx],
            send_sem=send_sem.at[row, zz],
            recv_sem=g_recv.at[row, idx],
            device_id=target,
            device_id_type=MESH,
        )

    def up_copy(buf, s, row, zz):
        return gather_copy(buf, s, row, zz, y, where_is(jnp.minimum(z + 1, nz - 1), y), g_up)

    def down_copy(buf, s, row, zz):
        return gather_copy(buf, s, row, zz, y, where_is(jnp.maximum(z - 1, 0), y), g_down)

    def side_copy(buf, s, row, zz, yy):
        return gather_copy(buf, s, row, zz, yy, where_is(z, other_y), g_side)

    def gather_start(buf, s, row):
        @pl.when(z < nz - 1)
        def _():
            up_copy(buf, s, row, z).start()

        @pl.when(z > 0)
        def _():
            down_copy(buf, s, row, z).start()

        side_copy(buf, s, row, z, y).start()

    def gather_step(buf, s, row, d):
        @pl.when(z - d >= 0)
        def _():
            zz = z - d
            side_copy(buf, s, row, zz, y).wait_recv()

            @pl.when(z < nz - 1)
            def _():
                up_copy(buf, s, row, zz).start()

            side_copy(buf, s, row, zz, y).start()

        @pl.when(z + d < nz)
        def _():
            zz = z + d
            side_copy(buf, s, row, zz, y).wait_recv()

            @pl.when(z > 0)
            def _():
                down_copy(buf, s, row, zz).start()

            side_copy(buf, s, row, zz, y).start()

    def gather_finish(buf, s, row):
        for zz in range(nz):
            side_copy(buf, s, row, zz, other_y).wait_recv()

    def gather_drain(buf, s, row):
        for zz in range(nz):
            side_copy(buf, s, row, zz, y).wait_send()

            @pl.when((zz <= z) & (z < nz - 1))
            def _():
                up_copy(buf, s, row, zz).wait_send()

            @pl.when((zz >= z) & (z > 0))
            def _():
                down_copy(buf, s, row, zz).wait_send()

    q_row = 1
    a_row = 1 + slices

    gather_start(info_buf, 0, 0)
    for s in range(slices):
        gather_start(q_buf, s, q_row + s)
    for b in range(blocks):
        kv_copies[b][0].start()
        kv_copies[b][1].start()
    weight_copy = pltpu.make_async_copy(weight_hbm, weight_buf, w_sem)
    weight_copy.start()
    for d in range(1, nz):
        gather_step(info_buf, 0, 0, d)
        gather_step(q_buf, 0, q_row, d)
    gather_finish(info_buf, 0, 0)

    info = info_buf[0].astype(F32).reshape(all_leaves, HEAD_SIZE)
    info_t = jnp.transpose(info)
    slots = info_t[0:8]
    last = info_t[8:9] + info_t[9:10]
    level = lax.broadcasted_iota(jnp.int32, (8, all_leaves), 0)
    lengths = jnp.where(level == 7, last, float(block_len))
    base = (me * blocks).astype(F32)
    first = lax.broadcasted_iota(jnp.int32, (8, all_leaves), 0)
    present = jnp.zeros((8, all_leaves), F32)
    valid = jnp.zeros((8, all_leaves), F32)
    for b in range(blocks):
        same = slots == base + float(b)
        here = jnp.sum(jnp.where(same, 1.0, 0.0), axis=0, keepdims=True)
        size = jnp.sum(jnp.where(same, lengths, 0.0), axis=0, keepdims=True)
        present = jnp.where(first == b, here, present)
        valid = jnp.where(first == b, size, valid)
    earlier = (
        lax.broadcasted_iota(jnp.int32, (all_leaves, all_leaves), 0)
        < lax.broadcasted_iota(jnp.int32, (all_leaves, all_leaves), 1)
    )
    rank = dot(present.astype(BF16), jnp.where(earlier, 1.0, 0.0).astype(BF16))
    rank = jnp.where(present > 0.5, rank, -1.0)
    ordinal = lax.broadcasted_iota(jnp.int32, (cap, all_leaves), 0).astype(F32)
    for b in range(blocks):
        chosen = jnp.where(ordinal == rank[b : b + 1], 1.0, 0.0)
        count[b] = jnp.broadcast_to(
            jnp.sum(chosen * valid[b : b + 1], axis=1, keepdims=True), (cap, HEAD_SIZE)
        )
        pick[b] = chosen.astype(BF16)
        pick_t[:, b * cap : (b + 1) * cap] = jnp.transpose(chosen).astype(BF16)

    lane_cap = lax.broadcasted_iota(jnp.int32, (cap, HEAD_SIZE), 1)
    position = lax.broadcasted_iota(jnp.int32, (PER_GROUP * cap, block_len), 1).astype(F32)
    ones = jnp.ones((block_len, HEAD_SIZE), BF16)

    def split_total(value):
        top = value.astype(BF16).astype(F32)
        return top, (value - top).astype(BF16).astype(F32)

    def pack_stats(reference, total):
        top, rest = split_total(total)
        lane = lax.broadcasted_iota(jnp.int32, reference.shape, 1)
        return jnp.where(
            lane < 32,
            reference,
            jnp.where(lane < 64, pltpu.roll(top, 32, 1), pltpu.roll(rest, 64, 1)),
        ).astype(BF16)

    def unpack_stats(stats):
        stats = stats.astype(F32)
        return stats, pltpu.roll(stats, 96, 1) + pltpu.roll(stats, 64, 1)

    def attend(s):
        if s == 0:
            for b in range(blocks):
                kv_copies[b][0].wait()
                kv_copies[b][1].wait()

        def score_block(b, highest):
            choose = pick[b]
            rows = dot(choose, q_buf[s].reshape(all_leaves, width)).astype(BF16)
            limit = count[b][:, 0:1]
            limit = jnp.concatenate([limit] * PER_GROUP, axis=0)
            inside = position < limit
            max_here = jnp.zeros((cap, HEAD_SIZE), F32)
            total_here = jnp.zeros((cap, HEAD_SIZE), F32)
            for g in range(sg):
                at = (s * sg + g) * HEAD_SIZE
                group_rows = jnp.concatenate(
                    [
                        rows[:, (g * PER_GROUP + e) * HEAD_SIZE : (g * PER_GROUP + e + 1) * HEAD_SIZE]
                        for e in range(PER_GROUP)
                    ],
                    axis=0,
                )
                scores = lax.dot_general(
                    group_rows,
                    key_buf[b, :, at : at + HEAD_SIZE],
                    (((1,), (1,)), ((), ())),
                    preferred_element_type=F32,
                )
                scores = jnp.where(inside, scores, NEG)
                top = jnp.max(scores, axis=1, keepdims=True)
                shares = jnp.exp2((scores - top) * scale2).astype(BF16)
                both = dot(
                    shares,
                    jnp.concatenate([value_buf[b, :, at : at + HEAD_SIZE], ones], axis=1),
                )
                sums = both[:, HEAD_SIZE:]
                unit = (both[:, :HEAD_SIZE] / sums).astype(BF16)
                scaled_top = top * scale
                for e in range(PER_GROUP):
                    h = g * PER_GROUP + e
                    unit_buf[b, :, h * HEAD_SIZE : (h + 1) * HEAD_SIZE] = unit[e * cap : (e + 1) * cap]
                    max_here = jnp.where(lane_cap == h, scaled_top[e * cap : (e + 1) * cap], max_here)
                    total_here = jnp.where(lane_cap == h, sums[e * cap : (e + 1) * cap], total_here)
            max_buf[b] = max_here
            total_buf[b] = total_here
            spread = lax.dot_general(
                choose,
                max_here.astype(BF16),
                (((0,), (0,)), ((), ())),
                preferred_element_type=F32,
            )
            have = lax.dot_general(
                choose,
                jnp.ones((cap, HEAD_SIZE), BF16),
                (((0,), (0,)), ((), ())),
                preferred_element_type=F32,
            )
            return jnp.maximum(highest, jnp.where(have > 0.5, spread, NEG))

        highest = lax.fori_loop(
            0, blocks, score_block, jnp.full((all_leaves, HEAD_SIZE), NEG, F32)
        )
        highest = highest.astype(BF16)

        def weigh_block(b, total):
            choose = pick[b]
            weight = jnp.exp(max_buf[b] - dot(choose, highest)) * total_buf[b]
            for h in range(heads):
                cols = slice(h * HEAD_SIZE, (h + 1) * HEAD_SIZE)
                unit_buf[b, :, cols] = (unit_buf[b, :, cols].astype(F32) * weight[:, h : h + 1]).astype(BF16)
            top, rest = split_total(weight)
            return total + lax.dot_general(
                choose,
                top.astype(BF16),
                (((0,), (0,)), ((), ())),
                preferred_element_type=F32,
            ) + lax.dot_general(
                choose,
                rest.astype(BF16),
                (((0,), (0,)), ((), ())),
                preferred_element_type=F32,
            )

        total = lax.fori_loop(0, blocks, weigh_block, jnp.zeros((all_leaves, HEAD_SIZE), F32))
        for g in range(sg):
            cols = slice(g * PER_GROUP * HEAD_SIZE, (g + 1) * PER_GROUP * HEAD_SIZE)
            num = dot(pick_t[...], unit_buf[:, :, cols].reshape(blocks * cap, PER_GROUP * HEAD_SIZE))
            part[s, :, :, cols] = num.astype(BF16).reshape(n, leaves, PER_GROUP * HEAD_SIZE)
        part[s, :, :, width:] = pack_stats(highest.astype(F32), total).reshape(n, leaves, HEAD_SIZE)

    def y_copy(s, zz):
        return pltpu.make_async_remote_copy(
            src_ref=part.at[s, zz * ROW_PAIR + other_y],
            dst_ref=y_recv.at[s, zz],
            send_sem=y_send_sem.at[s, zz],
            recv_sem=y_recv_sem.at[s, zz],
            device_id=where_is(z, other_y),
            device_id_type=MESH,
        )

    def y_start(s):
        for d in range(1, nz + 1):
            y_copy(s, (z + d) % nz).start()

    def z_copy(s, zz, slot):
        return pltpu.make_async_remote_copy(
            src_ref=merged.at[s, zz],
            dst_ref=z_recv.at[s, slot],
            send_sem=z_send_sem.at[s, zz],
            recv_sem=z_recv_sem.at[s, slot],
            device_id=where_is(zz, y),
            device_id_type=MESH,
        )

    def z_start(s):
        for d in range(1, nz + 1):
            zz = (z + d) % nz
            y_copy(s, zz).wait_recv()
            mine = zz * ROW_PAIR + y
            ref_a, tot_a = unpack_stats(part[s, mine, :, width:])
            ref_b, tot_b = unpack_stats(y_recv[s, zz, :, width:])
            ref = jnp.maximum(ref_a, ref_b)
            ea = jnp.exp(ref_a - ref)
            eb = jnp.exp(ref_b - ref)
            for h in range(heads):
                cols = slice(h * HEAD_SIZE, (h + 1) * HEAD_SIZE)
                merged[s, zz, :, cols] = (
                    part[s, mine, :, cols].astype(F32) * ea[:, h : h + 1]
                    + y_recv[s, zz, :, cols].astype(F32) * eb[:, h : h + 1]
                ).astype(BF16)
            merged[s, zz, :, width:] = pack_stats(ref, ea * tot_a + eb * tot_b)
            if d < nz:
                z_copy(s, zz, z).start()

    lane_leaf = lax.broadcasted_iota(jnp.int32, (leaves, HEAD_SIZE), 1)

    def finish(s):
        own = jnp.zeros((leaves, HEAD_SIZE), F32)
        for h in range(heads):
            at = (s * heads + h) * HEAD_SIZE
            kat = (s * sg + h // PER_GROUP) * HEAD_SIZE
            score = jnp.sum(
                q_ref[:, at : at + HEAD_SIZE].astype(F32) * nk_ref[:, kat : kat + HEAD_SIZE].astype(F32),
                axis=1,
                keepdims=True,
            )
            own = jnp.where(lane_leaf == h, score * scale, own)
        for d in range(1, nz):
            zz = (z + d) % nz
            z_copy(s, zz, zz).wait_recv()
        pieces = [(merged, z)] + [(z_recv, (z + d) % nz) for d in range(1, nz)]
        stats = [unpack_stats(buf[s, idx, :, width:]) for buf, idx in pieces]
        top = own
        for ref, _ in stats:
            top = jnp.maximum(top, ref)
        own_weight = jnp.exp(own - top)
        factors = [jnp.exp(ref - top) for ref, _ in stats]
        below = own_weight
        for factor, (_, tot) in zip(factors, stats):
            below = below + factor * tot
        inverse = 1.0 / below
        own_weight = own_weight * inverse
        factors = [factor * inverse for factor in factors]
        for h in range(heads):
            cols = slice(h * HEAD_SIZE, (h + 1) * HEAD_SIZE)
            kat = (s * sg + h // PER_GROUP) * HEAD_SIZE
            acc = own_weight[:, h : h + 1] * nv_ref[:, kat : kat + HEAD_SIZE].astype(F32)
            for factor, (buf, idx) in zip(factors, pieces):
                acc = acc + factor[:, h : h + 1] * buf[s, idx, :, cols].astype(F32)
            att_buf[s, me, :, cols] = acc.astype(BF16)

    for s in range(slices):
        if s > 0:
            for d in range(1, nz):
                gather_step(q_buf, s, q_row + s, d)
        gather_finish(q_buf, s, q_row + s)
        attend(s)
        y_start(s)
        if s >= 1:
            z_start(s - 1)
        if s >= 2:
            finish(s - 2)
            gather_start(att_buf, s - 2, a_row + s - 2)
    z_start(slices - 1)
    for s in range(max(slices - 2, 0), slices):
        finish(s)
        gather_start(att_buf, s, a_row + s)
    for s in range(slices):
        for d in range(1, nz):
            gather_step(att_buf, s, a_row + s, d)
    weight_copy.wait()
    half = n // 2
    rows = half * leaves
    for s in range(slices):
        gather_finish(att_buf, s, a_row + s)

    def project(start):
        acc = None
        for s in range(slices):
            piece = dot(
                att_buf[s, pl.ds(start, half)].reshape(rows, width),
                weight_buf[s * width : (s + 1) * width, :],
            )
            acc = piece if acc is None else acc + piece
        return acc

    half_send[...] = project((1 - core) * half)
    half_copy = pltpu.make_async_remote_copy(
        src_ref=half_send,
        dst_ref=half_recv,
        send_sem=h_send_sem,
        recv_sem=h_recv_sem,
        device_id=(parts_at, me, 1 - core),
        device_id_type=MESH,
    )
    half_copy.start()
    kept = project(core * half)

    gather_drain(info_buf, 0, 0)
    for s in range(slices):
        gather_drain(q_buf, s, q_row + s)
        gather_drain(att_buf, s, a_row + s)
        for d in range(1, nz + 1):
            y_copy(s, (z + d) % nz).wait_send()
        for d in range(1, nz):
            z_copy(s, (z + d) % nz, z).wait_send()
    half_copy.wait()
    out_ref[...] = (kept + half_recv[...]).astype(BF16)


def local(
    queries,
    block_key_cache,
    block_value_cache,
    new_keys,
    leaf_value_rows,
    ancestors,
    block_slot,
    last_len,
    o_weight,
):
    n = lax.axis_size("blk")
    leaves, features = queries.shape
    ancestry = ancestors.shape[1]
    blocks, block_len, kv_width = block_key_cache.shape
    block_count = blocks * n
    cap = 2 * leaves * ancestry // block_count * n
    slices = SLICES
    nz = n // ROW_PAIR
    heads = kv_width // HEAD_SIZE // slices * PER_GROUP
    width = heads * HEAD_SIZE
    packed = width + HEAD_SIZE
    columns = o_weight.shape[1]

    catalog = jnp.arange(block_count, dtype=jnp.int32)
    slot = jnp.sum(
        jnp.where(ancestors[:, :, None] == catalog, block_slot[None, None, :], 0), axis=2
    )
    low = jnp.minimum(last_len, 256)
    info = jnp.concatenate(
        [slot, low[:, None], (last_len - low)[:, None]], axis=1
    ).astype(BF16)
    info = jnp.pad(info, ((0, 0), (0, HEAD_SIZE - ancestry - 2)))

    vmem = pl.BlockSpec(memory_space=pltpu.VMEM)
    anywhere = pl.BlockSpec(memory_space=pl.ANY)
    dma = pltpu.SemaphoreType.DMA
    grows = 1 + 2 * slices
    return pl.pallas_call(
        functools.partial(kernel, n, slices, cap),
        out_shape=jax.ShapeDtypeStruct((n * leaves // 2, columns), BF16),
        in_specs=[vmem] * 4 + [anywhere] * 3,
        out_specs=vmem,
        scratch_shapes=[
            pltpu.VMEM((1, n, leaves, HEAD_SIZE), BF16),
            pltpu.VMEM((slices, n, leaves, width), BF16),
            pltpu.VMEM((blocks, block_len, kv_width), BF16),
            pltpu.VMEM((blocks, block_len, kv_width), BF16),
            pltpu.VMEM(o_weight.shape, BF16),
            pltpu.VMEM((blocks, cap, n * leaves), BF16),
            pltpu.VMEM((n * leaves, blocks * cap), BF16),
            pltpu.VMEM((blocks, cap, HEAD_SIZE), F32),
            pltpu.VMEM((blocks, cap, width), BF16),
            pltpu.VMEM((blocks, cap, HEAD_SIZE), F32),
            pltpu.VMEM((blocks, cap, HEAD_SIZE), F32),
            pltpu.VMEM((slices, n, leaves, packed), BF16),
            pltpu.VMEM((slices, nz, leaves, packed), BF16),
            pltpu.VMEM((slices, nz, leaves, packed), BF16),
            pltpu.VMEM((slices, nz, leaves, packed), BF16),
            pltpu.VMEM((slices, n, leaves, width), BF16),
            pltpu.VMEM((n * leaves // 2, columns), F32),
            pltpu.VMEM((n * leaves // 2, columns), F32),
            dma((2, blocks)),
            dma,
            dma((grows, n)),
            dma((grows, nz)),
            dma((grows, nz)),
            dma((grows, nz)),
            dma((slices, nz)),
            dma((slices, nz)),
            dma((slices, nz)),
            dma((slices, nz)),
            dma,
            dma,
        ],
        compiler_params=pltpu.CompilerParams(
            collective_id=0, has_side_effects=True, vmem_limit_bytes=56 * 1024 * 1024
        ),
        cost_estimate=pl.CostEstimate(
            flops=4_000_000_000, bytes_accessed=12_000_000, transcendentals=5_000_000
        ),
    )(
        queries,
        info,
        new_keys,
        leaf_value_rows,
        block_key_cache,
        block_value_cache,
        o_weight,
    )


def solution(mesh):
    return jax.shard_map(
        local,
        mesh=mesh,
        in_specs=(
            P(("parts", "blk"), "kvh"),
            P(("parts", "blk"), None, "kvh"),
            P(("parts", "blk"), None, "kvh"),
            P(("parts", "blk"), "kvh"),
            P(("parts", "blk"), "kvh"),
            P(("parts", "blk"), None),
            P("parts"),
            P(("parts", "blk")),
            P("kvh", "blk"),
        ),
        out_specs=P(("parts", "kvh"), "blk"),
        check_vma=False,
    )
```

time: 300 us -> 88.7 us (0.30)
  waiting for transfers between devices: 131 us -> 0 us
  Pallas kernels: 0 us -> 83.2 us
  local copies, waits for them, and re-layouts: 68.5 us -> 2.56 us
  matrix products: 33.8 us -> 0 us
  starting transfers between devices: 21.7 us -> 0 us
  other arithmetic: 19.8 us -> 2.68 us
  between operations: 13.6 us -> 0.02 us
  blocking collectives: 9.79 us -> 0 us
    pallas_call x0 -> x1, Pallas kernels: none -> 83.2 us  [local(): pl.pallas_call(functools.partial(kernel, n, slices, cap), out_shape=jax.S...]
    all_to_all x4 -> x0, waiting for transfers between devices: 83 us -> none  [the longest x1 44.8 us: local(): lax.all_to_all(outgoing, 'blk', split_axis=0, concat_axis=0, tiled=True)]
    all_gather x1 -> x0, waiting for transfers between devices: 40.9 us -> none  [local(): lax.all_gather(attention, 'blk', axis=0, tiled=True)]
    dot_general x18 -> x0, matrix products: 33.8 us -> none  [the longest x8 15.2 us: one_block(): jnp.einsum('gscek,kgh->scgeh', shares, value_part, preferred_element_type...]
    all_to_all x4 -> x0, starting transfers between devices: 21.4 us -> none  [the longest x1 7.28 us: local(): lax.all_to_all(length_flat.reshape(devices_blk, local_blocks * capacity),...]
    gather x6 -> x0, local copies, waits for them, and re-layouts: 18 us -> none  [the longest x1 7.06 us: local(): queries[leaf_index].reshape(devices_blk, local_blocks * capacity, features)]
    unnamed x13 -> x2, local copies, waits for them, and re-layouts: 16.1 us -> 2.36 us
    dynamic_update_slice x16 -> x0, local copies, waits for them, and re-layouts: 12.3 us -> none  [owner_attention(): lax.map(one_block, (arranged, counted, gathered_keys, gathered_values))]
  transfers between devices with their start and end apart: 6 -> 0, of which waited for: 5 -> 0; matrix products, arithmetic and copies ran while one was open for 16% -> 0% of each run, Pallas kernels for 0% -> 0%
where the time goes in v1:
time: 88.7 us; the launch traced here: 88.5 us
  Pallas kernels  83.2 us (94%)
  other arithmetic  2.68 us (3%)
  local copies, waits for them, and re-layouts  2.56 us (3%)
    pallas_call x1, Pallas kernels, local(): pl.pallas_call(functools.partial(kernel, n, slices, cap), out_shape=jax.S...  83.2 us
    unnamed x2, local copies, waits for them, and re-layouts  2.36 us

profile of v1, /device:TPU:0, one launch (start us, length us, event | category | flops | bytes accessed | tf_op | source)
XLA Modules:
  0.0 88.5 jit_solution(10403807239019769470)
XLA Ops:
  0.0 0.7 fusion.5
  0.7 0.1 copy.14
  0.8 0.1 copy.15
  0.9 0.8 copy.13
  1.6 1.3 %select_reduce_fusion = s32[32,8]{1,0:T(8,128)S(1)} fusion(s32[64]{0:T(128)} %param.15, s32[32,8]{1,0:T(8,128)S(1)} %copy.13), kind=kLoop, calls=%fused_computation | loop fusion | flops 48896 | bytes 2304 | tf_op jit(solution)/shard_map/reduce_sum | solution.py:506
  3.0 0.7 fusion.4.info_ref
  3.7 83.2 %shard_map.91 = bf16[128,640]{1,0:T(8,128)(2,1)} custom-call(bf16[32,2560]{1,0:T(8,128)(2,1)} %q_ref.1, bf16[32,128]{1,0:T(8,128)(2,1)} %fusion.4.info_ref, bf16[32,512]{1,0:T(8,128)(2,1)} %nk_ref.1, bf16[32,512]{1,0:T(8,128)(2,1)} %nv_ref.1, bf16[8,512,512]{2,1,0:T(8,128)(2,1)} %key_hbm.1, bf16[8,512,512]{2,1,0:T(8,128)(2,1)} %value_hbm.1, ...), custom_call_target="tpu_custom_call" | custom-call | flops 4000000000 | bytes 12000000 | tf_op jit(solution)/shard_map/pallas_call | solution.py:519
  86.9 1.6 %copy.17 = bf16[128,640]{1,0:T(8,128)(2,1)} copy(bf16[128,640]{1,0:T(8,128)(2,1)} %shard_map.91) | data formatting | bytes 327680
  (1 shorter events, 0.0 us)

commit v2 on v1

--- a/solution.py
+++ b/solution.py
@@ -13,7 +13,8 @@
 HEAD_SIZE = 128
 PER_GROUP = QUERY_HEADS // KEY_VALUE_HEADS
 ROW_PAIR = 2
-SLICES = 1
+SLICES = 2
+UNROLL = 8
 NEG = -1e30
 MESH = pl.DeviceIdType.MESH
 F32 = jnp.float32
@@ -29,7 +30,9 @@
     slices,
     cap,
     q_ref,
-    info_ref,
+    path_ref,
+    last_ref,
+    slot_ref,
     nk_ref,
     nv_ref,
     key_hbm,
@@ -43,6 +46,7 @@
     weight_buf,
     pick,
     pick_t,
+    pick_m,
     count,
     unit_buf,
     max_buf,
@@ -53,6 +57,7 @@
     z_recv,
     att_buf,
     half_send,
+    half_keep,
     half_recv,
     kv_sem,
     w_sem,
@@ -96,7 +101,9 @@
             )
         )
 
-    info_buf[0, me] = info_ref[...]
+    info_buf[0, me] = jnp.zeros((16, HEAD_SIZE), jnp.int32)
+    info_buf[0, me, 0:8, 0:leaves] = path_ref[...]
+    info_buf[0, me, 8:9, 0:leaves] = last_ref[...]
     for s in range(slices):
         q_buf[s, me] = q_ref[:, s * width : (s + 1) * width]
 
@@ -182,9 +189,15 @@
     q_row = 1
     a_row = 1 + slices
 
+    def query_wave(w):
+        if w < slices:
+            gather_start(q_buf, w, q_row + w)
+        for s in range(slices):
+            if 1 <= w - s < nz:
+                gather_step(q_buf, s, q_row + s, w - s)
+
     gather_start(info_buf, 0, 0)
-    for s in range(slices):
-        gather_start(q_buf, s, q_row + s)
+    query_wave(0)
     for b in range(blocks):
         kv_copies[b][0].start()
         kv_copies[b][1].start()
@@ -192,21 +205,22 @@
     weight_copy.start()
     for d in range(1, nz):
         gather_step(info_buf, 0, 0, d)
-        gather_step(q_buf, 0, q_row, d)
+        query_wave(d)
     gather_finish(info_buf, 0, 0)
 
-    info = info_buf[0].astype(F32).reshape(all_leaves, HEAD_SIZE)
-    info_t = jnp.transpose(info)
-    slots = info_t[0:8]
-    last = info_t[8:9] + info_t[9:10]
+    info_t = jnp.concatenate([info_buf[0, i, :, 0:leaves] for i in range(n)], axis=1)
+    path = info_t[0:8]
+    last = info_t[8:9].astype(F32)
     level = lax.broadcasted_iota(jnp.int32, (8, all_leaves), 0)
     lengths = jnp.where(level == 7, last, float(block_len))
-    base = (me * blocks).astype(F32)
+    slot_of = slot_ref[...]
+    block_id = lax.broadcasted_iota(jnp.int32, slot_of.shape, 1)
     first = lax.broadcasted_iota(jnp.int32, (8, all_leaves), 0)
     present = jnp.zeros((8, all_leaves), F32)
     valid = jnp.zeros((8, all_leaves), F32)
     for b in range(blocks):
-        same = slots == base + float(b)
+        mine = jnp.sum(jnp.where(slot_of == me * blocks + b, block_id, 0), axis=1, keepdims=True)
+        same = path == mine
         here = jnp.sum(jnp.where(same, 1.0, 0.0), axis=0, keepdims=True)
         size = jnp.sum(jnp.where(same, lengths, 0.0), axis=0, keepdims=True)
         present = jnp.where(first == b, here, present)
@@ -224,11 +238,18 @@
             jnp.sum(chosen * valid[b : b + 1], axis=1, keepdims=True), (cap, HEAD_SIZE)
         )
         pick[b] = chosen.astype(BF16)
-        pick_t[:, b * cap : (b + 1) * cap] = jnp.transpose(chosen).astype(BF16)
+        back = jnp.transpose(chosen)
+        pick_t[:, b * cap : (b + 1) * cap] = back.astype(BF16)
+        missing = 1.0 - jnp.sum(back, axis=1, keepdims=True)
+        spot = lax.broadcasted_iota(jnp.int32, (all_leaves, HEAD_SIZE - cap), 1)
+        pick_m[b] = jnp.concatenate([back, jnp.where(spot == 0, missing, 0.0)], axis=1).astype(BF16)
 
     lane_cap = lax.broadcasted_iota(jnp.int32, (cap, HEAD_SIZE), 1)
     position = lax.broadcasted_iota(jnp.int32, (PER_GROUP * cap, block_len), 1).astype(F32)
     ones = jnp.ones((block_len, HEAD_SIZE), BF16)
+    floor_rows = jnp.where(
+        lax.broadcasted_iota(jnp.int32, (HEAD_SIZE - cap, HEAD_SIZE), 0) == 0, NEG, 0.0
+    ).astype(BF16)
 
     def split_total(value):
         top = value.astype(BF16).astype(F32)
@@ -247,7 +268,7 @@
         stats = stats.astype(F32)
         return stats, pltpu.roll(stats, 96, 1) + pltpu.roll(stats, 64, 1)
 
-    def attend(s):
+    def score(s):
         if s == 0:
             for b in range(blocks):
                 kv_copies[b][0].wait()
@@ -293,49 +314,32 @@
                     total_here = jnp.where(lane_cap == h, sums[e * cap : (e + 1) * cap], total_here)
             max_buf[b] = max_here
             total_buf[b] = total_here
-            spread = lax.dot_general(
-                choose,
-                max_here.astype(BF16),
-                (((0,), (0,)), ((), ())),
-                preferred_element_type=F32,
-            )
-            have = lax.dot_general(
-                choose,
-                jnp.ones((cap, HEAD_SIZE), BF16),
-                (((0,), (0,)), ((), ())),
-                preferred_element_type=F32,
-            )
-            return jnp.maximum(highest, jnp.where(have > 0.5, spread, NEG))
+            spread = dot(pick_m[b], jnp.concatenate([max_here.astype(BF16), floor_rows], axis=0))
+            return jnp.maximum(highest, spread)
 
         highest = lax.fori_loop(
-            0, blocks, score_block, jnp.full((all_leaves, HEAD_SIZE), NEG, F32)
-        )
-        highest = highest.astype(BF16)
-
-        def weigh_block(b, total):
-            choose = pick[b]
-            weight = jnp.exp(max_buf[b] - dot(choose, highest)) * total_buf[b]
+            0, blocks, score_block, jnp.full((all_leaves, HEAD_SIZE), NEG, F32), unroll=UNROLL
+        )
+        return highest.astype(BF16)
+
+    def weigh(s, highest):
+        def weigh_block(b, carry):
+            weight = jnp.exp(max_buf[b] - dot(pick[b], highest)) * total_buf[b]
             for h in range(heads):
                 cols = slice(h * HEAD_SIZE, (h + 1) * HEAD_SIZE)
                 unit_buf[b, :, cols] = (unit_buf[b, :, cols].astype(F32) * weight[:, h : h + 1]).astype(BF16)
             top, rest = split_total(weight)
-            return total + lax.dot_general(
-                choose,
-                top.astype(BF16),
-                (((0,), (0,)), ((), ())),
-                preferred_element_type=F32,
-            ) + lax.dot_general(
-                choose,
-                rest.astype(BF16),
-                (((0,), (0,)), ((), ())),
-                preferred_element_type=F32,
-            )
-
-        total = lax.fori_loop(0, blocks, weigh_block, jnp.zeros((all_leaves, HEAD_SIZE), F32))
+            unit_buf[b, :, width : width + HEAD_SIZE] = top.astype(BF16)
+            unit_buf[b, :, width + HEAD_SIZE :] = rest.astype(BF16)
+            return carry
+
+        lax.fori_loop(0, blocks, weigh_block, 0, unroll=UNROLL)
         for g in range(sg):
             cols = slice(g * PER_GROUP * HEAD_SIZE, (g + 1) * PER_GROUP * HEAD_SIZE)
             num = dot(pick_t[...], unit_buf[:, :, cols].reshape(blocks * cap, PER_GROUP * HEAD_SIZE))
             part[s, :, :, cols] = num.astype(BF16).reshape(n, leaves, PER_GROUP * HEAD_SIZE)
+        total = dot(pick_t[...], unit_buf[:, :, width:].reshape(blocks * cap, 2 * HEAD_SIZE))
+        total = total[:, :HEAD_SIZE] + total[:, HEAD_SIZE:]
         part[s, :, :, width:] = pack_stats(highest.astype(F32), total).reshape(n, leaves, HEAD_SIZE)
 
     def y_copy(s, zz):
@@ -419,42 +423,60 @@
                 acc = acc + factor[:, h : h + 1] * buf[s, idx, :, cols].astype(F32)
             att_buf[s, me, :, cols] = acc.astype(BF16)
 
+    half = n // 2
+    rows = half * leaves
+    end = slices - 1
+
+    def att_wave(w):
+        if w < slices:
+            finish(w)
+            gather_start(att_buf, w, a_row + w)
+        for s in range(slices):
+            if 1 <= w - s < nz:
+                gather_step(att_buf, s, a_row + s, w - s)
+
+    def project(s, start):
+        return dot(
+            att_buf[s, pl.ds(start, half)].reshape(rows, width),
+            weight_buf[s * width : (s + 1) * width, :],
+        )
+
+    def project_both(s):
+        gather_finish(att_buf, s, a_row + s)
+        sent = project(s, (1 - core) * half)
+        own = project(s, core * half)
+        half_send[...] = sent if s == 0 else half_send[...] + sent
+        half_keep[...] = own if s == 0 else half_keep[...] + own
+
+    wave = nz
+    query_wave(wave)
     for s in range(slices):
-        if s > 0:
-            for d in range(1, nz):
-                gather_step(q_buf, s, q_row + s, d)
+        if s == slices - 1:
+            for w in range(wave + 1, slices + nz - 1):
+                query_wave(w)
         gather_finish(q_buf, s, q_row + s)
-        attend(s)
-        y_start(s)
+        highest = score(s)
+        if s < slices - 2:
+            wave = wave + 1
+            if wave < slices + nz - 1:
+                query_wave(wave)
+        if s >= 2:
+            att_wave(s - 2)
         if s >= 1:
             z_start(s - 1)
-        if s >= 2:
-            finish(s - 2)
-            gather_start(att_buf, s - 2, a_row + s - 2)
-    z_start(slices - 1)
-    for s in range(max(slices - 2, 0), slices):
-        finish(s)
-        gather_start(att_buf, s, a_row + s)
-    for s in range(slices):
-        for d in range(1, nz):
-            gather_step(att_buf, s, a_row + s, d)
+        weigh(s, highest)
+        y_start(s)
     weight_copy.wait()
-    half = n // 2
-    rows = half * leaves
-    for s in range(slices):
-        gather_finish(att_buf, s, a_row + s)
-
-    def project(start):
-        acc = None
-        for s in range(slices):
-            piece = dot(
-                att_buf[s, pl.ds(start, half)].reshape(rows, width),
-                weight_buf[s * width : (s + 1) * width, :],
-            )
-            acc = piece if acc is None else acc + piece
-        return acc
-
-    half_send[...] = project((1 - core) * half)
+    for w in range(max(slices - 2, 0), end):
+        att_wave(w)
+    z_start(end)
+    for w in range(end, slices + nz - 1):
+        att_wave(w)
+        if 0 <= w - nz < end:
+            project_both(w - nz)
+    gather_finish(att_buf, end, a_row + end)
+    sent = project(end, (1 - core) * half)
+    half_send[...] = sent if end == 0 else half_send[...] + sent
     half_copy = pltpu.make_async_remote_copy(
         src_ref=half_send,
         dst_ref=half_recv,
@@ -464,7 +486,9 @@
         device_id_type=MESH,
     )
     half_copy.start()
-    kept = project(core * half)
+    kept = project(end, core * half)
+    if end > 0:
+        kept = kept + half_keep[...]
 
     gather_drain(info_buf, 0, 0)
     for s in range(slices):
@@ -502,16 +526,6 @@
     packed = width + HEAD_SIZE
     columns = o_weight.shape[1]
 
-    catalog = jnp.arange(block_count, dtype=jnp.int32)
-    slot = jnp.sum(
-        jnp.where(ancestors[:, :, None] == catalog, block_slot[None, None, :], 0), axis=2
-    )
-    low = jnp.minimum(last_len, 256)
-    info = jnp.concatenate(
-        [slot, low[:, None], (last_len - low)[:, None]], axis=1
-    ).astype(BF16)
-    info = jnp.pad(info, ((0, 0), (0, HEAD_SIZE - ancestry - 2)))
-
     vmem = pl.BlockSpec(memory_space=pltpu.VMEM)
     anywhere = pl.BlockSpec(memory_space=pl.ANY)
     dma = pltpu.SemaphoreType.DMA
@@ -519,18 +533,19 @@
     return pl.pallas_call(
         functools.partial(kernel, n, slices, cap),
         out_shape=jax.ShapeDtypeStruct((n * leaves // 2, columns), BF16),
-        in_specs=[vmem] * 4 + [anywhere] * 3,
+        in_specs=[vmem] * 6 + [anywhere] * 3,
         out_specs=vmem,
         scratch_shapes=[
-            pltpu.VMEM((1, n, leaves, HEAD_SIZE), BF16),
+            pltpu.VMEM((1, n, 16, HEAD_SIZE), jnp.int32),
             pltpu.VMEM((slices, n, leaves, width), BF16),
             pltpu.VMEM((blocks, block_len, kv_width), BF16),
             pltpu.VMEM((blocks, block_len, kv_width), BF16),
             pltpu.VMEM(o_weight.shape, BF16),
             pltpu.VMEM((blocks, cap, n * leaves), BF16),
             pltpu.VMEM((n * leaves, blocks * cap), BF16),
+            pltpu.VMEM((blocks, n * leaves, HEAD_SIZE), BF16),
             pltpu.VMEM((blocks, cap, HEAD_SIZE), F32),
-            pltpu.VMEM((blocks, cap, width), BF16),
+            pltpu.VMEM((blocks, cap, width + 2 * HEAD_SIZE), BF16),
             pltpu.VMEM((blocks, cap, HEAD_SIZE), F32),
             pltpu.VMEM((blocks, cap, HEAD_SIZE), F32),
             pltpu.VMEM((slices, n, leaves, packed), BF16),
@@ -538,6 +553,7 @@
             pltpu.VMEM((slices, nz, leaves, packed), BF16),
             pltpu.VMEM((slices, nz, leaves, packed), BF16),
             pltpu.VMEM((slices, n, leaves, width), BF16),
+            pltpu.VMEM((n * leaves // 2, columns), F32),
             pltpu.VMEM((n * leaves // 2, columns), F32),
             pltpu.VMEM((n * leaves // 2, columns), F32),
             dma((2, blocks)),
@@ -561,7 +577,9 @@
         ),
     )(
         queries,
-        info,
+        ancestors.T,
+        last_len[None, :],
+        block_slot[None, :],
         new_keys,
         leaf_value_rows,
         block_key_cache,

time: 88.7 us -> 71.4 us (0.80)
  Pallas kernels: 83.2 us -> 69.7 us
  other arithmetic: 2.68 us -> 0 us
  local copies, waits for them, and re-layouts: 2.56 us -> 1.6 us
    pallas_call x1, Pallas kernels: 83.2 us -> 69.7 us  [local(): pl.pallas_call(functools.partial(kernel, n, slices, cap), out_shape=jax.S...]
    reduce_sum x1 -> x0, other arithmetic: 1.34 us -> none  [local(): jnp.sum(jnp.where(ancestors[:, :, None] == catalog, block_slot[None, None...]
    unnamed x2 -> x1, local copies, waits for them, and re-layouts: 2.36 us -> 1.6 us
where the time goes in v2:
time: 71.4 us; the launch traced here: 71.3 us
  Pallas kernels  69.7 us (98%)
  local copies, waits for them, and re-layouts  1.6 us (2%)
    pallas_call x1, Pallas kernels, local(): pl.pallas_call(functools.partial(kernel, n, slices, cap), out_shape=jax.S...  69.7 us
    unnamed x1, local copies, waits for them, and re-layouts  1.6 us

profile of v2, /device:TPU:0, one launch (start us, length us, event | category | flops | bytes accessed | tf_op | source)
XLA Modules:
  0.0 71.3 jit_solution(6274399953218473894)
XLA Ops:
  0.0 69.7 %shard_map.91 = bf16[128,640]{1,0:T(8,128)(2,1)} custom-call(bf16[32,2560]{1,0:T(8,128)(2,1)} %q_ref.1, s32[8,32]{1,0:T(8,128)} %bitcast.3, s32[1,32]{1,0:T(1,128)} %bitcast.4, s32[1,64]{1,0:T(1,128)} %bitcast.5, bf16[32,512]{1,0:T(8,128)(2,1)} %nk_ref.1, bf16[32,512]{1,0:T(8,128)(2,1)} %nv_ref.1, bf16[8,512,512]{2,1,0:T(8,128)(2,1)} %key_hbm.1, ...), custom_call_target="tpu_custom_call" | custom-call | flops 4000000000 | bytes 12000000 | tf_op jit(solution)/shard_map/pallas_call | solution.py:533
  69.7 1.6 %copy.11 = bf16[128,640]{1,0:T(8,128)(2,1)} copy(bf16[128,640]{1,0:T(8,128)(2,1)} %shard_map.91) | data formatting | bytes 327680

commit v3 on v2

--- a/solution.py
+++ b/solution.py
@@ -468,8 +468,10 @@
         y_start(s)
     weight_copy.wait()
     for w in range(max(slices - 2, 0), end):
-        att_wave(w)
+        finish(w)
     z_start(end)
+    for w in range(max(slices - 2, 0), end):
+        gather_start(att_buf, w, a_row + w)
     for w in range(end, slices + nz - 1):
         att_wave(w)
         if 0 <= w - nz < end:

time: 71.4 us -> 70.5 us (0.987)
  Pallas kernels: 69.7 us -> 68.7 us
    pallas_call x1, Pallas kernels: 69.7 us -> 68.7 us  [local(): pl.pallas_call(functools.partial(kernel, n, slices, cap), out_shape=jax.S...]
where the time goes in v3:
time: 70.5 us; the launch traced here: 70.3 us
  Pallas kernels  68.7 us (97%)
  local copies, waits for them, and re-layouts  1.6 us (2%)
    pallas_call x1, Pallas kernels, local(): pl.pallas_call(functools.partial(kernel, n, slices, cap), out_shape=jax.S...  68.7 us
    unnamed x1, local copies, waits for them, and re-layouts  1.6 us

profile of v3, /device:TPU:0, one launch (start us, length us, event | category | flops | bytes accessed | tf_op | source)
XLA Modules:
  0.0 70.3 jit_solution(10605832660393335479)
XLA Ops:
  0.0 68.7 %shard_map.91 = bf16[128,640]{1,0:T(8,128)(2,1)} custom-call(bf16[32,2560]{1,0:T(8,128)(2,1)} %q_ref.1, s32[8,32]{1,0:T(8,128)} %bitcast.3, s32[1,32]{1,0:T(1,128)} %bitcast.4, s32[1,64]{1,0:T(1,128)} %bitcast.5, bf16[32,512]{1,0:T(8,128)(2,1)} %nk_ref.1, bf16[32,512]{1,0:T(8,128)(2,1)} %nv_ref.1, bf16[8,512,512]{2,1,0:T(8,128)(2,1)} %key_hbm.1, ...), custom_call_target="tpu_custom_call" | custom-call | flops 4000000000 | bytes 12000000 | tf_op jit(solution)/shard_map/pallas_call | solution.py:535
  68.7 1.6 %copy.11 = bf16[128,640]{1,0:T(8,128)(2,1)} copy(bf16[128,640]{1,0:T(8,128)(2,1)} %shard_map.91) | data formatting | bytes 327680
